TPU v7x, 256 devices: a whole 4x4x8 slice. The times are simulated.
256 devices in a mesh: vox: 8 (over x, core), mem: 32 (over y, z).
Axes of the slice: x: 4, y: 4, z: 8, core: 2. Of those that a mesh axis runs over, the one named last changes fastest.
Arguments:
- ensemble: bfloat16 [256, 524288], P('mem', 'vox'), may hold values from -6 to 6
- partials: float32 [8, 256, 131072], P('vox', 'mem'), may hold values from -6 to 6
- perturb: float32 [256, 131072], P('mem', 'vox'), may hold values from -6 to 6
- observed: float32 [131072], P('vox'), may hold values from -6 to 6
- variance: float32 [131072], P('vox'), may hold values from 0.5 to 2
- obs_lists: int32 [4096, 64], P(('vox', 'mem')), may hold values from 0 to 127, all different within a row
- taper_index: int32 [4096, 64], P(('vox', 'mem')), may hold values from 0 to 15
- taper_table: float32 [16], replicated, may hold values from 0.1 to 1
Outputs:
- updated: bfloat16 [256, 524288], P('mem', 'vox')
All inputs are finite; a program needn't handle non-finite values.
Results may differ from a plain program's by a relative error of at most 0.017.
Values may be sent and summed in bfloat16 or wider, within the bound.
A program may use at most 128 MiB of HBM per device.

v0:
```python
import jax
import jax.numpy as jnp
from jax import lax
from jax.sharding import PartitionSpec as P

OB = 128


def center(values):
    as_float = values.astype(jnp.float32)
    return (as_float - jnp.mean(as_float, axis=0, keepdims=True)).astype(jnp.bfloat16)


def block_moments(obs_anom, weights):
    return jnp.einsum("kbi,lbi->bkl", obs_anom, weights, preferred_element_type=jnp.float32)


def from_moments(moments, coeff, state_anom):
    high = lax.Precision.HIGHEST
    combined = jnp.einsum("bo,okl->bkl", coeff, moments, precision=high).astype(jnp.bfloat16)
    return jnp.einsum("kbc,bkl->lbc", state_anom, combined, preferred_element_type=jnp.float32)


def local(ensemble, partials, perturb, observed, variance, obs_lists, taper_index, taper_table):
    summed = lax.psum_scatter(
        partials[0].astype(jnp.bfloat16), "vox", scatter_dimension=1, tiled=True
    )
    weights = (
        (observed[None, :] + perturb - summed.astype(jnp.float32)) / variance[None, :]
    ).astype(jnp.bfloat16)
    members = lax.all_to_all(ensemble, "mem", split_axis=1, concat_axis=0, tiled=True)
    count = members.shape[0]
    blocks = obs_lists.shape[0]
    cells = members.shape[1] // blocks
    groups = weights.shape[1] // OB
    state_anom = center(members).reshape(count, blocks, cells)
    table_hits = (
        taper_index[:, :, None] == jnp.arange(taper_table.shape[0], dtype=jnp.int32)[None, None, :]
    ).astype(jnp.float32)
    tapers = jnp.sum(table_hits * taper_table[None, None, :], axis=2)
    picks = (obs_lists[:, :, None] == jnp.arange(groups, dtype=jnp.int32)[None, None, :]).astype(
        jnp.float32
    )
    coeff = jnp.sum(tapers[:, :, None] * picks, axis=1)
    pred_all, wts_all = (
        lax.all_gather(summed, "mem", axis=0, tiled=True),
        lax.all_gather(weights, "mem", axis=0, tiled=True),
    )
    obs_anom = center(pred_all).reshape(count, groups, OB)
    moments = block_moments(obs_anom, wts_all.reshape(count, groups, OB))
    increment = from_moments(moments, coeff, state_anom).reshape(count, blocks * cells)
    updated = (members.astype(jnp.float32) + increment * (1.0 / (count - 1))).astype(jnp.bfloat16)
    return lax.all_to_all(updated, "mem", split_axis=0, concat_axis=1, tiled=True)


def solution(mesh):
    return jax.shard_map(
        local,
        mesh=mesh,
        in_specs=(
            P("mem", "vox"),
            P("vox", "mem", None),
            P("mem", "vox"),
            P("vox"),
            P("vox"),
            P(("vox", "mem"), None),
            P(("vox", "mem"), None),
            P(),
        ),
        out_specs=P("mem", "vox"),
        check_vma=False,
    )
```

profile of v0, /device:TPU:2, one launch (start us, length us, event | category | flops | bytes accessed | tf_op | source)
XLA Modules:
  0.0 376.0 jit_solution(18339346806040277107)
XLA Ops:
  6.5 0.0 copy-start
  6.5 0.0 copy-start.2
  6.5 0.0 copy-start.1
  6.5 0.0 reduce-scatter.2.cloned.1.call-start
  6.5 3.8 %convert_bitcast_fusion.2 = bf16[8,131072]{1,0:T(8,128)(2,1)} fusion(f32[1,8,131072]{2,1,0:T(8,128)} %param.9), kind=kLoop, calls=%fused_computation.19 | loop fusion | flops 1048576 | bytes 6291456 | tf_op jit(solution)/shard_map/convert_element_type | solution.py:26
  10.3 0.0 copy-start.4
  10.3 0.0 copy-start.5
  10.3 0.0 copy-start.3
  10.3 0.0 reduce-scatter.2.cloned.1.call-update
  10.4 0.0 all-gather.3.cloned.1.call-start
  10.4 36.0 %reduce-scatter.2.cloned.1.call-done = bf16[8,16384]{1,0:T(8,128)(2,1)} async-done(((bf16[8,131072]{1,0:T(8,128)(2,1)}), bf16[8,16384]{1,0:T(8,128)(2,1)}) %reduce-scatter.2.cloned.1.call-update) | async-done | bytes 262160 | tf_op jit(solution)/shard_map/reduce_scatter | solution.py:25
  46.4 0.0 all-gather.3.cloned.1.call-update
  46.4 0.0 all-gather.5.cloned.1.call-start
  46.5 0.0 copy-done
  46.5 0.0 copy-done.2
  46.5 0.0 copy-done.1
  46.5 1.8 divide_convert_fusion
  48.3 0.0 all-gather.5.cloned.1.call-update
  48.3 9.8 %all-to-all-start = ((bf16[8,32,2048]{2,0,1:T(8,128)(2,1)}), bf16[8,32,2048]{2,0,1:T(8,128)(2,1)S(1)}, u32[]{:S(2)}, u32[]{:S(2)}) async-start(bf16[8,32,2048]{2,0,1:T(8,128)(2,1)} %bitcast), calls=%async_computation | async-start | bytes 2097152 | tf_op jit(solution)/shard_map/all_to_all | solution.py:31
  58.1 0.0 copy-done.4
  58.1 0.0 copy-done.5
  58.1 0.1 select_reduce_fusion.1
  58.2 0.0 copy-done.3
  58.2 0.3 select_reduce_fusion
  58.6 32.4 %all-to-all-done = bf16[8,32,2048]{2,0,1:T(8,128)(2,1)S(1)} async-done(((bf16[8,32,2048]{2,0,1:T(8,128)(2,1)}), bf16[8,32,2048]{2,0,1:T(8,128)(2,1)S(1)}, u32[]{:S(2)}, u32[]{:S(2)}) %all-to-all-start) | async-done | bytes 1048608 | tf_op jit(solution)/shard_map/all_to_all | solution.py:31
  91.0 0.2 convert_bitcast_fusion
  91.3 0.4 copy.36
  91.7 0.2 convert_reduce_fusion.1
  91.8 0.2 fusion.9
  92.0 65.0 %all-gather.3.cloned.1.call-done = bf16[256,16384]{1,0:T(8,128)(2,1)} async-done(((bf16[8,16384]{1,0:T(8,128)(2,1)}), bf16[256,16384]{1,0:T(8,128)(2,1)}) %all-gather.3.cloned.1.call-update) | async-done | bytes 8388624 | tf_op jit(solution)/shard_map/all_gather | solution.py:46
  157.0 4.8 %convert_reduce_fusion = f32[16384]{0:T(1024)S(1)} fusion(bf16[256,16384]{1,0:T(8,128)(2,1)} %all-gather.3.cloned.1.call-done), kind=kLoop, calls=%fused_computation.3 | loop fusion | flops 8372224 | bytes 8454144 | tf_op jit(solution)/shard_map/reduce_sum | solution.py:11
  161.8 93.4 %all-gather.5.cloned.1.call-done = bf16[256,16384]{1,0:T(8,128)(2,1)} async-done(((bf16[8,16384]{1,0:T(8,128)(2,1)}), bf16[256,16384]{1,0:T(8,128)(2,1)}) %all-gather.5.cloned.1.call-update) | async-done | bytes 8388624 | tf_op jit(solution)/shard_map/all_gather | solution.py:47
  255.2 11.9 %copy.27 = bf16[256,16384]{0,1:T(8,128)(2,1)} copy(bf16[256,16384]{1,0:T(8,128)(2,1)} %all-gather.5.cloned.1.call-done) | data formatting | bytes 16777216 | tf_op jit(solution)/shard_map/all_gather | solution.py:47
  267.2 17.8 %fusion.4 = f32[128,256,256]{2,1,0:T(8,128)} fusion(bf16[256,128,128]{0,2,1:T(8,128)(2,1)} %bitcast.35, bf16[256,16384]{1,0:T(8,128)(2,1)} %all-gather.3.cloned.1.call-done, f32[16384]{0:T(1024)S(1)} %broadcast_multiply_fusion), kind=kOutput, calls=%fused_computation.6 | convolution fusion | flops 2160066560 | bytes 50397184 | tf_op jit(solution)/shard_map/kbi,lbi->bkl/dot_general | solution.py:15
  284.9 43.5 %fusion.12 = bf16[16,256,256]{2,0,1:T(8,128)(2,1)S(1)} fusion(f32[128,256,256]{2,1,0:T(8,128)} %fusion.4, f32[16,128]{1,0:T(8,128)S(1)} %select_reduce_fusion), kind=kOutput, calls=%fused_computation.20 | convolution fusion | flops 1611661312 | bytes 35659776 | tf_op jit(solution)/shard_map/bo,okl->bkl/dot_general | solution.py:20
  328.5 1.7 multiply_bitcast_fusion
  330.1 2.6 copy.33
  332.7 1.7 mul.36
  334.4 0.3 fusion.8
  334.7 33.8 %all_to_all.29 = bf16[32,8,2048]{2,1,0:T(8,128)(2,1)S(1)} all-to-all(bf16[32,8,2048]{2,1,0:T(8,128)(2,1)S(1)} %fusion.8), channel_id=1, replica_groups=mesh['vox'=8,'mem'=32] {'mem'}, dimensions={0} | all-to-all | bytes 2097152 | tf_op jit(solution)/shard_map/all_to_all | solution.py:53
  368.5 1.0 copy.52
  (2 shorter events, 0.0 us)
Async XLA Ops:
  6.5 39.9 %copy-start = (f32[8,16384]{1,0:T(8,128)S(1)}, f32[8,16384]{1,0:T(8,128)}, u32[]{:S(2)}) copy-start(f32[8,16384]{1,0:T(8,128)} %param.10) | copy-start | bytes 1572868
  6.5 40.0 %copy-start.2 = (f32[16384]{0:T(1024)S(1)}, f32[16384]{0:T(1024)}, u32[]{:S(2)}) copy-start(f32[16384]{0:T(1024)} %param.11) | copy-start | bytes 196612
  6.5 40.0 %copy-start.1 = (f32[16384]{0:T(1024)S(1)}, f32[16384]{0:T(1024)}, u32[]{:S(2)}) copy-start(f32[16384]{0:T(1024)} %param.12) | copy-start | bytes 196612
  6.5 39.9 %reduce-scatter.2.cloned.1.call-start = ((), (), s32[]{:S(2)}) async-start(), calls=%async_computation.3 | async-start | bytes 2359296 | tf_op jit(solution)/shard_map/reduce_scatter | solution.py:25
  10.3 47.8 %copy-start.4 = (s32[16,64]{1,0:T(8,128)S(1)}, s32[16,64]{1,0:T(8,128)}, u32[]{:S(2)}) copy-start(s32[16,64]{1,0:T(8,128)} %param.14) | copy-start | bytes 12292
  10.3 47.8 %copy-start.5 = (f32[16]{0:T(128)S(1)}, f32[16]{0:T(128)}, u32[]{:S(2)}) copy-start(f32[16]{0:T(128)} %param.15) | copy-start | bytes 196
  10.3 47.9 %copy-start.3 = (s32[16,64]{1,0:T(8,128)S(1)}, s32[16,64]{1,0:T(8,128)}, u32[]{:S(2)}) copy-start(s32[16,64]{1,0:T(8,128)} %param.13) | copy-start | bytes 12292
  10.4 146.7 %all-gather.3.cloned.1.call-start = ((), (), s32[]{:S(2)}) async-start(), calls=%async_computation.4 | async-start | bytes 8650752 | tf_op jit(solution)/shard_map/all_gather | solution.py:46
  46.4 208.8 %all-gather.5.cloned.1.call-start = ((), (), s32[]{:S(2)}) async-start(), calls=%async_computation.5 | async-start | bytes 8650752 | tf_op jit(solution)/shard_map/all_gather | solution.py:47
  48.3 42.7 %all-to-all-start = ((bf16[8,32,2048]{2,0,1:T(8,128)(2,1)}), bf16[8,32,2048]{2,0,1:T(8,128)(2,1)S(1)}, u32[]{:S(2)}, u32[]{:S(2)}) async-start(bf16[8,32,2048]{2,0,1:T(8,128)(2,1)} %bitcast), calls=%async_computation | async-start | bytes 2097152 | tf_op jit(solution)/shard_map/all_to_all | solution.py:31
Sparse Core Ops, SparseCore 0:
  10.5 35.8 reduce-scatter.1
  49.0 107.9 all-gather.2
  159.6 95.5 all-gather.4
where the time goes:
time: 377 us; the launch traced here: 376 us
  waiting for transfers between devices  227 us (60%)
  matrix products  63 us (17%)
  blocking collectives  33.8 us (9%)
  local copies, waits for them, and re-layouts  17.6 us (5%)
  between operations  13.3 us (4%)
  other arithmetic  11.6 us (3%)
  starting transfers between devices  9.9 us (3%)
    all_gather x1, waiting for transfers between devices, local(): lax.all_gather(weights, 'mem', axis=0, tiled=True)  93.4 us
    all_gather x1, waiting for transfers between devices, local(): lax.all_gather(summed, 'mem', axis=0, tiled=True)  65 us
    dot_general x1, matrix products, from_moments(): jnp.einsum('bo,okl->bkl', coeff, moments, precision=high)  43.5 us
    reduce_scatter x1, waiting for transfers between devices, local(): lax.psum_scatter(partials[0].astype(jnp.bfloat16), 'vox', scatter_dimensi...  36 us
    all_to_all x1, blocking collectives, local(): lax.all_to_all(updated, 'mem', split_axis=0, concat_axis=1, tiled=True)  33.8 us
    all_to_all x1, waiting for transfers between devices, local(): lax.all_to_all(ensemble, 'mem', split_axis=1, concat_axis=0, tiled=True)  32.4 us
    dot_general x1, matrix products, block_moments(): jnp.einsum('kbi,lbi->bkl', obs_anom, weights, preferred_element_type=jnp....  17.8 us
    all_gather x1, local copies, waits for them, and re-layouts, local(): lax.all_gather(weights, 'mem', axis=0, tiled=True)  11.9 us
  transfers between devices with their start and end apart: 4, of which 4 were waited for; matrix products, arithmetic and copies ran while one was open for 2% of the time, Pallas kernels for 0%

commit v1 on v0

--- a/solution.py
+++ b/solution.py
@@ -28,7 +28,10 @@
     weights = (
         (observed[None, :] + perturb - summed.astype(jnp.float32)) / variance[None, :]
     ).astype(jnp.bfloat16)
-    members = lax.all_to_all(ensemble, "mem", split_axis=1, concat_axis=0, tiled=True)
+    members = jnp.concatenate(
+        lax.all_to_all(jnp.stack(jnp.split(ensemble, lax.axis_size("mem"), axis=1)), "mem", 0, 0),
+        axis=0,
+    )
     count = members.shape[0]
     blocks = obs_lists.shape[0]
     cells = members.shape[1] // blocks

time: 377 us -> 377 us (level)
  waiting for transfers between devices: 227 us -> 207 us
  local copies, waits for them, and re-layouts: 17.6 us -> 37.3 us
    unnamed x14 -> x47, local copies, waits for them, and re-layouts: 1.38 us -> 20.5 us
    all_gather x1, waiting for transfers between devices: 65 us -> 46.5 us  [local(): lax.all_gather(summed, 'mem', axis=0, tiled=True)]
  transfers between devices with their start and end apart: 4 -> 4, of which waited for: 4 -> 4; matrix products, arithmetic and copies ran while one was open for 2% -> 7% of each run, Pallas kernels for 0% -> 0%
where the time goes in v1:
time: 377 us; the launch traced here: 376 us
  waiting for transfers between devices  207 us (55%)
  matrix products  63.2 us (17%)
  local copies, waits for them, and re-layouts  37.3 us (10%)
  blocking collectives  33.8 us (9%)
  between operations  13.3 us (4%)
  other arithmetic  11.5 us (3%)
  starting transfers between devices  9.92 us (3%)
    all_gather x1, waiting for transfers between devices, local(): lax.all_gather(weights, 'mem', axis=0, tiled=True)  93.4 us
    all_gather x1, waiting for transfers between devices, local(): lax.all_gather(summed, 'mem', axis=0, tiled=True)  46.5 us
    dot_general x1, matrix products, from_moments(): jnp.einsum('bo,okl->bkl', coeff, moments, precision=high)  43.5 us
    reduce_scatter x1, waiting for transfers between devices, local(): lax.psum_scatter(partials[0].astype(jnp.bfloat16), 'vox', scatter_dimensi...  36 us
    all_to_all x1, blocking collectives, local(): lax.all_to_all(updated, 'mem', split_axis=0, concat_axis=1, tiled=True)  33.8 us
    all_to_all x1, waiting for transfers between devices, local(): lax.all_to_all(jnp.stack(jnp.split(ensemble, lax.axis_size('mem'), axis=1...  31.3 us
    unnamed x47, local copies, waits for them, and re-layouts  20.5 us
    dot_general x1, matrix products, block_moments(): jnp.einsum('kbi,lbi->bkl', obs_anom, weights, preferred_element_type=jnp....  17.7 us
  transfers between devices with their start and end apart: 4, of which 4 were waited for; matrix products, arithmetic and copies ran while one was open for 7% of the time, Pallas kernels for 0%

profile of v1, /device:TPU:2, one launch (start us, length us, event | category | flops | bytes accessed | tf_op | source)
XLA Modules:
  0.0 376.3 jit_solution(1157940055044112627)
XLA Ops:
  6.6 3.8 %convert_bitcast_fusion.1 = bf16[8,131072]{1,0:T(8,128)(2,1)} fusion(f32[1,8,131072]{2,1,0:T(8,128)} %param.9), kind=kLoop, calls=%fused_computation.18 | loop fusion | flops 1048576 | bytes 6291456 | tf_op jit(solution)/shard_map/convert_element_type | solution.py:26
  10.5 36.0 %reduce-scatter.2.cloned.1.call-done = bf16[8,16384]{1,0:T(8,128)(2,1)} async-done(((bf16[8,131072]{1,0:T(8,128)(2,1)}), bf16[8,16384]{1,0:T(8,128)(2,1)}) %reduce-scatter.2.cloned.1.call-update) | async-done | bytes 262160 | tf_op jit(solution)/shard_map/reduce_scatter | solution.py:25
  46.6 0.6 constant_dynamic-update-slice_fusion.31
  47.2 0.6 constant_dynamic-update-slice_fusion.30
  47.8 0.6 constant_dynamic-update-slice_fusion.29
  48.4 0.6 constant_dynamic-update-slice_fusion.28
  49.1 1.8 divide_convert_fusion
  50.8 0.6 constant_dynamic-update-slice_fusion.27
  51.5 0.6 constant_dynamic-update-slice_fusion.26
  52.1 0.6 constant_dynamic-update-slice_fusion.25
  52.7 0.6 constant_dynamic-update-slice_fusion.24
  53.3 0.6 constant_dynamic-update-slice_fusion.23
  53.9 0.6 constant_dynamic-update-slice_fusion.22
  54.5 0.6 constant_dynamic-update-slice_fusion.21
  55.2 0.6 constant_dynamic-update-slice_fusion.20
  55.8 0.6 constant_dynamic-update-slice_fusion.19
  56.4 0.6 constant_dynamic-update-slice_fusion.18
  57.0 0.6 constant_dynamic-update-slice_fusion.17
  57.6 0.6 constant_dynamic-update-slice_fusion.16
  58.2 0.6 constant_dynamic-update-slice_fusion.15
  58.9 0.6 constant_dynamic-update-slice_fusion.14
  59.5 0.6 constant_dynamic-update-slice_fusion.13
  60.1 0.6 constant_dynamic-update-slice_fusion.12
  60.7 0.6 constant_dynamic-update-slice_fusion.11
  61.3 0.6 constant_dynamic-update-slice_fusion.10
  62.0 0.6 constant_dynamic-update-slice_fusion.9
  62.6 0.6 constant_dynamic-update-slice_fusion.8
  63.2 0.6 constant_dynamic-update-slice_fusion.7
  63.8 0.6 constant_dynamic-update-slice_fusion.6
  64.4 0.6 constant_dynamic-update-slice_fusion.5
  65.0 0.6 constant_dynamic-update-slice_fusion.4
  65.7 0.6 constant_dynamic-update-slice_fusion.3
  66.3 0.6 constant_dynamic-update-slice_fusion.2
  66.9 0.6 constant_dynamic-update-slice_fusion.1
  67.5 0.6 constant_dynamic-update-slice_fusion
  68.1 9.8 %all-to-all-start = ((bf16[32,8,2048]{2,1,0:T(8,128)(2,1)}), bf16[32,8,2048]{2,1,0:T(8,128)(2,1)S(1)}, u32[]{:S(2)}, u32[]{:S(2)}) async-start(bf16[32,8,2048]{2,1,0:T(8,128)(2,1)} %constant_dynamic-update-slice_fusion), calls=%async_computation | async-start | bytes 2097152 | tf_op jit(solution)/shard_map/all_to_all | solution.py:32
  78.4 31.3 %all-to-all-done = bf16[32,8,2048]{2,1,0:T(8,128)(2,1)S(1)} async-done(((bf16[32,8,2048]{2,1,0:T(8,128)(2,1)}), bf16[32,8,2048]{2,1,0:T(8,128)(2,1)S(1)}, u32[]{:S(2)}, u32[]{:S(2)}) %all-to-all-start) | async-done | bytes 1048608 | tf_op jit(solution)/shard_map/all_to_all | solution.py:32
  110.6 46.5 %all-gather.3.cloned.1.call-done = bf16[256,16384]{1,0:T(8,128)(2,1)} async-done(((bf16[8,16384]{1,0:T(8,128)(2,1)}), bf16[256,16384]{1,0:T(8,128)(2,1)}) %all-gather.3.cloned.1.call-update) | async-done | bytes 8388624 | tf_op jit(solution)/shard_map/all_gather | solution.py:49
  157.1 4.8 %convert_reduce_fusion = f32[16384]{0:T(1024)S(1)} fusion(bf16[256,16384]{1,0:T(8,128)(2,1)} %all-gather.3.cloned.1.call-done), kind=kLoop, calls=%fused_computation.3 | loop fusion | flops 8372224 | bytes 8454144 | tf_op jit(solution)/shard_map/reduce_sum | solution.py:11
  161.9 93.4 %all-gather.5.cloned.1.call-done = bf16[256,16384]{1,0:T(8,128)(2,1)} async-done(((bf16[8,16384]{1,0:T(8,128)(2,1)}), bf16[256,16384]{1,0:T(8,128)(2,1)}) %all-gather.5.cloned.1.call-update) | async-done | bytes 8388624 | tf_op jit(solution)/shard_map/all_gather | solution.py:50
  255.3 11.9 %copy.28 = bf16[256,16384]{0,1:T(8,128)(2,1)} copy(bf16[256,16384]{1,0:T(8,128)(2,1)} %all-gather.5.cloned.1.call-done) | data formatting | bytes 16777216 | tf_op jit(solution)/shard_map/all_gather | solution.py:50
  267.2 17.7 %fusion.4 = f32[128,256,256]{2,1,0:T(8,128)} fusion(bf16[256,128,128]{0,2,1:T(8,128)(2,1)} %bitcast.89, bf16[256,16384]{1,0:T(8,128)(2,1)} %all-gather.3.cloned.1.call-done, f32[16384]{0:T(1024)S(1)} %broadcast_multiply_fusion), kind=kOutput, calls=%fused_computation.6 | convolution fusion | flops 2160066560 | bytes 50397184 | tf_op jit(solution)/shard_map/kbi,lbi->bkl/dot_general | solution.py:15
  284.9 43.5 %fusion.11 = bf16[16,256,256]{2,0,1:T(8,128)(2,1)S(1)} fusion(f32[128,256,256]{2,1,0:T(8,128)} %fusion.4, f32[16,128]{1,0:T(8,128)S(1)} %select_reduce_fusion), kind=kOutput, calls=%fused_computation.19 | convolution fusion | flops 1611661312 | bytes 35659776 | tf_op jit(solution)/shard_map/bo,okl->bkl/dot_general | solution.py:20
  328.5 2.0 multiply_bitcast_fusion
  330.5 2.5 copy.34
  333.0 1.7 mul.36
  335.0 33.8 %all_to_all.21 = bf16[32,8,2048]{2,1,0:T(8,128)(2,1)S(1)} all-to-all(bf16[32,8,2048]{2,1,0:T(8,128)(2,1)S(1)} %fusion.7), channel_id=1, replica_groups=mesh['vox'=8,'mem'=32] {'mem'}, dimensions={0} | all-to-all | bytes 2097152 | tf_op jit(solution)/shard_map/all_to_all | solution.py:56
  368.8 1.0 copy.86
  (28 shorter events, 1.7 us)
Async XLA Ops:
  6.5 40.0 %copy-start = (bf16[8,65536]{1,0:T(8,128)(2,1)S(1)}, bf16[8,65536]{1,0:T(8,128)(2,1)}, u32[]{:S(2)}) copy-start(bf16[8,65536]{1,0:T(8,128)(2,1)} %param.8) | copy-start | bytes 3145732
  6.5 42.5 %copy-start.1 = (f32[8,16384]{1,0:T(8,128)S(1)}, f32[8,16384]{1,0:T(8,128)}, u32[]{:S(2)}) copy-start(f32[8,16384]{1,0:T(8,128)} %param.10) | copy-start | bytes 1572868
  6.5 42.5 %copy-start.3 = (f32[16384]{0:T(1024)S(1)}, f32[16384]{0:T(1024)}, u32[]{:S(2)}) copy-start(f32[16384]{0:T(1024)} %param.11) | copy-start | bytes 196612
  6.5 42.5 %copy-start.2 = (f32[16384]{0:T(1024)S(1)}, f32[16384]{0:T(1024)}, u32[]{:S(2)}) copy-start(f32[16384]{0:T(1024)} %param.12) | copy-start | bytes 196612
  6.5 40.0 %reduce-scatter.2.cloned.1.call-start = ((), (), s32[]{:S(2)}) async-start(), calls=%async_computation.3 | async-start | bytes 2359296 | tf_op jit(solution)/shard_map/reduce_scatter | solution.py:25
  10.4 67.5 %copy-start.5 = (s32[16,64]{1,0:T(8,128)S(1)}, s32[16,64]{1,0:T(8,128)}, u32[]{:S(2)}) copy-start(s32[16,64]{1,0:T(8,128)} %param.14) | copy-start | bytes 12292
  10.4 67.5 %copy-start.6 = (f32[16]{0:T(128)S(1)}, f32[16]{0:T(128)}, u32[]{:S(2)}) copy-start(f32[16]{0:T(128)} %param.15) | copy-start | bytes 196
  10.4 67.6 %copy-start.4 = (s32[16,64]{1,0:T(8,128)S(1)}, s32[16,64]{1,0:T(8,128)}, u32[]{:S(2)}) copy-start(s32[16,64]{1,0:T(8,128)} %param.13) | copy-start | bytes 12292
  10.5 146.6 %all-gather.3.cloned.1.call-start = ((), (), s32[]{:S(2)}) async-start(), calls=%async_computation.4 | async-start | bytes 8650752 | tf_op jit(solution)/shard_map/all_gather | solution.py:49
  46.5 208.8 %all-gather.5.cloned.1.call-start = ((), (), s32[]{:S(2)}) async-start(), calls=%async_computation.5 | async-start | bytes 8650752 | tf_op jit(solution)/shard_map/all_gather | solution.py:50
  68.1 41.6 %all-to-all-start = ((bf16[32,8,2048]{2,1,0:T(8,128)(2,1)}), bf16[32,8,2048]{2,1,0:T(8,128)(2,1)S(1)}, u32[]{:S(2)}, u32[]{:S(2)}) async-start(bf16[32,8,2048]{2,1,0:T(8,128)(2,1)} %constant_dynamic-update-slice_fusion), calls=%async_computation | async-start | bytes 2097152 | tf_op jit(solution)/shard_map/all_to_all | solution.py:32
Sparse Core Ops, SparseCore 0:
  10.6 35.8 reduce-scatter.1
  49.1 107.9 all-gather.2
  159.7 95.5 all-gather.4
